TPU v7x, 256 devices: a whole 4x4x8 slice. The times are simulated.
256 devices in a mesh: row: 32 (over z, x_lo, core), col: 8 (over y, x_hi).
Axes of the slice: x: 4 (x_hi: 2, x_lo: 2; x = x_hi * 2 + x_lo), y: 4, z: 8, core: 2. Of those that a mesh axis runs over, the one named last changes fastest.
Arguments:
- noise_draw: bfloat16 [16384, 4096], P('row', 'col'), may hold values from -6 to 6
- latent_code: bfloat16 [4096, 4096], P('col', 'row'), may hold values from -6 to 6
- start_potential: float32 [4096], P('col'), may hold values from -0.6 to 0.6
Outputs:
- noise_potential: float32 [16384], P('row')
- latent_potential: float32 [4096], P('col')
- transported: float32 [4096, 4096], P('row', 'col')
All inputs are finite; a program needn't handle non-finite values.
Results may differ from a plain program's by a relative error of at most 0.0028.
Values may be sent and summed in bfloat16 or wider, within the bound.
A program may use at most 128 MiB of HBM per device.

v0:
```python
import math

import jax
import jax.numpy as jnp
from jax import lax
from jax.experimental import pallas as pl
from jax.experimental.pallas import tpu as pltpu
from jax.sharding import PartitionSpec as P

ITERS = 3
EPS = 0.01
LOG2E = math.log2(math.e)
MESH = pl.DeviceIdType.MESH
F32 = jnp.float32
BF16 = jnp.bfloat16

Z, Y = 8, 4
LANE = 128
BLK = 512
HALF = BLK // 2


def kernel(
    n_total, m_total, width,
    noise_ref, latent_ref, start_ref,
    npot_ref, lpot_ref, out_ref,
    nz, lt, no, relay, cross, nsq, lsq, wt, wx, nx, part, parth, stage, land, stageh, landh, xs, xr, rowx, col2,
    n_send, n_recv, h_send, h_recv, l_send, l_recv, o_send, o_recv, w_send, w_recv,
    p_send, p_recv, r_send, r_recv, c2_send, c2_recv,
    s_send, s_recv, t_send, t_recv, x_send, x_recv, loc,
):
    row = lax.axis_index("row")
    col = lax.axis_index("col")
    z = row // 4
    xl = (row // 2) % 2
    core = row % 2
    y = col // 2
    xh = col % 2
    quad = row % 4

    def ring_z(d):
        return (z + d + Z) % Z

    def ring_y(d):
        return (y + d + Y) % Y

    other_core = (row + 1 - 2 * core, col)
    other_xl = (row + 2 - 4 * xl, col)
    flip_col = col + 1 - 2 * xh
    diagonal = (row + 2 - 4 * xl, flip_col)
    z_up = (ring_z(1) * 4 + quad, col)
    z_dn = (ring_z(-1) * 4 + quad, col)
    y_up = (row, ring_y(1) * 2 + xh)
    y_dn = (row, ring_y(-1) * 2 + xh)
    col_peers = [
        (row, ring_y(dy) * 2 + (1 - xh if dx else xh))
        for dy, dx in ((2, 1), (1, 1), (-1, 1), (2, 0), (0, 1), (1, 0), (-1, 0))
    ]
    across = (row + 2 - 4 * xl) // 2 * 2
    across_quad = ((across + 1 - core) % 4, (across + core) % 4, (quad // 2) * 2 + 1 - core, quad)
    row_peers = [
        (ring_z(d) * 4 + q, col)
        for d in (4, 3, -3, 2, -2, 1, -1, 0) for q in across_quad[:3 if d == 0 else 4]
    ]
    peers = col_peers + row_peers + [(across, flip_col), (across + 1, flip_col)]

    own_n = pltpu.make_async_copy(noise_ref, nz.at[col], loc.at[0])
    own_l = pltpu.make_async_copy(latent_ref, lt.at[z, core, xl], loc.at[1])
    own_n.start()
    own_l.start()

    barrier = pltpu.get_barrier_semaphore()
    for peer in peers:
        pl.semaphore_signal(barrier, inc=1, device_id=peer, device_id_type=MESH)
    cross[...] = jnp.zeros_like(cross)
    nsq[...] = jnp.zeros_like(nsq)
    lsq[...] = jnp.zeros_like(lsq)
    pl.semaphore_wait(barrier, len(peers))

    def rc(src, dst, ssem, rsem, dev):
        return pltpu.make_async_remote_copy(
            src_ref=src, dst_ref=dst, send_sem=ssem, recv_sem=rsem,
            device_id=dev, device_id_type=MESH,
        )

    def nsl(slot, h):
        return nz.at[slot, pl.ds(h * HALF, HALF), :]

    sent = []

    def nsend(slot, h, idx, dev, src=None):
        src = nsl(slot, h) if src is None else src
        c = rc(src, nsl(slot, h), n_send.at[idx], n_recv.at[idx], dev)
        c.start()
        return c

    def own_half(h):
        return noise_ref.at[pl.ds(h * HALF, HALF), :]

    def nwait(slot, h, idx):
        rc(nsl(slot, h), nsl(slot, h), n_send.at[idx], n_recv.at[idx], y_up).wait_recv()

    def lsend(ref, idx, dev, src=None):
        c = rc(ref if src is None else src, ref, l_send.at[idx], l_recv.at[idx], dev)
        c.start()
        sent.append(c)

    def lwait(ref, idx):
        rc(ref, ref, l_send.at[idx], l_recv.at[idx], z_up).wait_recv()

    QUART = HALF // 2

    def slot_of(yy, s):
        return yy * 2 + (xh if s == 0 else 1 - xh)

    def quarter(slot, path, p):
        return nz.at[slot, pl.ds(path * HALF + p * QUART, QUART), :]

    def relay_start(t, path, p):
        if t == 0:
            ref = noise_ref.at[pl.ds(path * HALF + p * QUART, QUART), :]
        else:
            ref = quarter(slot_of(ring_y(2), 0), path, p)
        c = rc(ref, relay.at[t, path, p], h_send.at[0, t, path, p], h_recv.at[0, t, path, p],
               other_xl if path == 0 else diagonal)
        c.start()
        sent.append(c)

    def relay_forward(t, path, p):
        ref = quarter(slot_of(ring_y(2 * t), path), path, p)
        dev = diagonal if path == 0 else other_xl
        buf = relay.at[t, path, p]
        rc(buf, buf, h_send.at[0, t, path, p], h_recv.at[0, t, path, p], dev).wait_recv()
        c = rc(buf, ref, h_send.at[1, t, path, p], h_recv.at[1, t, path, p], dev)
        c.start()
        sent.append(c)

    def relay_end(t, path):
        for p in range(2):
            ref = quarter(slot_of(ring_y(2 * t), 1), path, p)
            rc(ref, ref, h_send.at[1, t, path, p], h_recv.at[1, t, path, p], diagonal).wait_recv()

    own_pair = lt.at[z, core]
    own_block = lt.at[z, core, xl]
    lsend(own_block, 0, other_xl, latent_ref)
    for p in range(2):
        relay_start(0, 0, p)
        relay_start(0, 1, p)
    sent.append(nsend(col, 0, 0, y_up, own_half(0)))
    sent.append(nsend(col, 1, 3, y_dn, own_half(1)))
    lsend(own_block, 1, z_up, latent_ref)
    lsend(own_block, 6, z_dn, latent_ref)

    lwait(lt.at[z, core, 1 - xl], 0)
    lsend(lt.at[z, core, 1 - xl], 2, z_up)
    lsend(lt.at[z, core, 1 - xl], 7, z_dn)
    own_l.wait()
    lsend(own_pair, 11, other_core)

    dn, up = slot_of(ring_y(-1), 0), slot_of(ring_y(1), 0)
    nwait(dn, 0, 0)
    onward_up = nsend(dn, 0, 4, y_up)
    nwait(up, 1, 3)
    onward_dn = nsend(up, 1, 5, y_dn)
    for p in range(2):
        relay_forward(0, 0, p)
        relay_forward(0, 1, p)

    for sgn, base, dev in ((-1, 1, z_up), (1, 6, z_dn)):
        zz = ring_z(sgn)
        lwait(lt.at[zz, core, xl], base)
        lwait(lt.at[zz, core, 1 - xl], base + 1)
        lsend(lt.at[zz, core], base + 2, dev)
        lsend(lt.at[zz, core], 12 + (base == 6), other_core)

    onward_up.wait_send()
    sent.append(nsend(col, 1, 1, y_up, own_half(1)))
    onward_dn.wait_send()
    sent.append(nsend(col, 0, 2, y_dn, own_half(0)))

    nwait(slot_of(ring_y(2), 0), 0, 4)
    relay_start(1, 0, 0)
    relay_start(1, 0, 1)
    nwait(slot_of(ring_y(2), 0), 1, 5)
    relay_start(1, 1, 0)
    relay_start(1, 1, 1)

    for sgn, base, dev in ((-1, 1, z_up), (1, 6, z_dn)):
        zz = ring_z(2 * sgn)
        lwait(lt.at[zz, core], base + 2)
        lsend(lt.at[zz, core], base + 3, dev)
        lsend(lt.at[zz, core], 14 + (base == 6), other_core)

    relay_end(0, 0)
    sent.append(nsend(flip_col, 0, 6, y_up))
    sent.append(nsend(flip_col, 0, 8, y_dn))
    relay_end(0, 1)
    sent.append(nsend(flip_col, 1, 9, y_dn))
    sent.append(nsend(flip_col, 1, 7, y_up))

    for sgn, base, dev in ((-1, 1, z_up), (1, 6, z_dn)):
        zz = ring_z(3 * sgn)
        lwait(lt.at[zz, core], base + 3)
        lsend(lt.at[zz, core, int(base == 6)], base + 4, dev)
        lsend(lt.at[zz, core], 16 + (base == 6), other_core)
    far = ring_z(4)
    lwait(lt.at[far, core, 0], 5)
    lwait(lt.at[far, core, 1], 10)
    lsend(lt.at[far, core], 18, other_core)
    for p in range(2):
        for path in range(2):
            relay_forward(1, path, p)
    for j, d in enumerate((0, -1, 1, -2, 2, -3, 3, 4)):
        lwait(lt.at[ring_z(d), 1 - core], 11 + j)

    def accumulate(slot):
        a = nz[slot]
        b = jnp.concatenate([lt[slot, 0, 0], lt[slot, 1, 0], lt[slot, 0, 1], lt[slot, 1, 1]], axis=1)
        cross[...] += lax.dot_general(a, b, (((1,), (1,)), ((), ())), preferred_element_type=F32)
        a2 = jnp.square(a.astype(F32))
        nsq[...] += (a2[:, 0:128] + a2[:, 128:256]) + (a2[:, 256:384] + a2[:, 384:512])
        b2 = jnp.square(b.astype(F32))
        lsq[...] += (b2[:, 0:128] + b2[:, 128:256]) + (b2[:, 256:384] + b2[:, 384:512])

    def wait_rest(s):
        dn, up = slot_of(ring_y(-1), s), slot_of(ring_y(1), s)
        nwait(dn, 1, 6 * s + 1)
        nwait(up, 0, 6 * s + 2)

    own_n.wait()
    wait_rest(0)

    def set0(k, carry):
        accumulate(((y + k) % Y) * 2 + xh)
        return carry

    lax.fori_loop(0, Y, set0, 0)
    accumulate(flip_col)
    relay_end(1, 0)
    relay_end(1, 1)
    accumulate(slot_of(ring_y(2), 1))
    dn, up = slot_of(ring_y(-1), 1), slot_of(ring_y(1), 1)
    nwait(dn, 0, 6)
    nwait(up, 1, 9)
    wait_rest(1)
    accumulate(dn)
    accumulate(up)

    for q in range(2):
        c = rc(
            nz.at[:, :, pl.ds(pl.multiple_of(q * 256 + (1 - core) * LANE, LANE), LANE)],
            no.at[:, :, pl.ds(q * LANE, LANE)],
            o_send.at[q], o_recv.at[q], other_core,
        )
        c.start()
        sent.append(c)

    eye = (
        lax.broadcasted_iota(jnp.int32, (LANE, LANE), 0)
        == lax.broadcasted_iota(jnp.int32, (LANE, LANE), 1)
    )

    def to_lanes(v):
        return jnp.sum(jnp.where(eye, v, 0.0), axis=0, keepdims=True)

    def to_rows(v):
        return jnp.sum(jnp.where(eye, v, 0.0), axis=1, keepdims=True)

    def wide(v):
        return jnp.concatenate([v[q:q + 1, :] for q in range(4)], axis=1)

    scale = LOG2E / (width * EPS)
    lq = jnp.concatenate(
        [to_lanes(jnp.sum(lsq[q * LANE:(q + 1) * LANE, :], axis=1, keepdims=True)) for q in range(4)],
        axis=1,
    )
    for b in range(4):
        rows = slice(b * LANE, (b + 1) * LANE)
        nq = jnp.sum(nsq[rows, :], axis=1, keepdims=True)
        cross[rows, :] = (nq + lq - 2.0 * cross[rows, :]) * scale

    def merge(parts):
        best = jnp.max(parts, axis=0)
        return best + jnp.log2(jnp.sum(jnp.exp2(parts - best[None]), axis=0))

    def merge_rows(parts):
        best = jnp.max(parts, axis=0, keepdims=True)
        return best + jnp.log2(jnp.sum(jnp.exp2(parts - best), axis=0, keepdims=True))

    def lend(step):
        k, zz = step % 2, step // 2
        lanes = pl.ds(pl.multiple_of((1 - xl) * 256 + k * LANE, LANE), LANE)
        for slot, dev in ((zz, (across + k, col)), (zz + 4, (across + k, flip_col))):
            c = rc(nz.at[slot, :, lanes], nx.at[core, slot], p_send.at[k, slot], p_recv.at[core, slot], dev)
            c.start()
            sent.append(c)

    steps = iter(range(6))

    def exchange(buf, mine, peers, ssem, rsem):
        for peer in peers:
            rc(buf.at[mine], buf.at[mine], ssem, rsem, peer).start()
        step = next(steps)
        for piece_at in range(step * 8 // 6, (step + 1) * 8 // 6):
            lend(piece_at)
        k = len(peers)
        rc(buf.at[pl.ds(0, k)], buf.at[pl.ds(0, k)], ssem, rsem, peers[0]).wait_recv()

    g = start_ref[...] * (LOG2E / EPS)
    f = None
    f_rows = None
    for it in range(ITERS):
        for b in range(4):
            parts = []
            for r in range(b * LANE, (b + 1) * LANE, 32):
                s = [g[q:q + 1, :] - cross[r:r + 32, q * LANE:(q + 1) * LANE] for q in range(4)]
                top = jnp.maximum(jnp.maximum(s[0], s[1]), jnp.maximum(s[2], s[3]))
                e = [jnp.exp2(v - top) for v in s]
                parts.append(top + jnp.log2((e[0] + e[1]) + (e[2] + e[3])))
            rowx[it, col, b:b + 1, :] = merge_rows(jnp.concatenate(parts, axis=0).T)
        exchange(rowx.at[it], col, col_peers, r_send.at[it], r_recv.at[it])
        f = -(math.log2(m_total) + merge(rowx[it]))
        f_rows = [to_rows(f[b:b + 1, :]) for b in range(4)]
        parts = []
        for r in range(0, BLK, 64):
            fr = f_rows[r // LANE][r % LANE:r % LANE + 64]
            s = (fr - cross[r:r + 64, :]).reshape(8, 8, BLK)
            top = jnp.max(s, axis=0)
            parts.append(top + jnp.log2(jnp.sum(jnp.exp2(s - top[None]), axis=0)))
        top = parts[0]
        for v in parts[1:]:
            top = jnp.maximum(top, v)
        own = merge_rows(top + jnp.log2(sum(jnp.exp2(v - top) for v in parts)))
        for q in range(4):
            col2[it, row, q:q + 1, :] = own[:, q * LANE:(q + 1) * LANE]
        exchange(col2.at[it], row, row_peers, c2_send.at[it], c2_recv.at[it])
        g = -(math.log2(n_total) + merge(col2[it]))

    npot_ref[...] = f * (EPS / LOG2E)
    lpot_ref[...] = g * (EPS / LOG2E)

    LOW, HIGH = slice(0, HALF), slice(HALF, BLK)
    gw = wide(g)

    def weights(cols):
        for b in range(4):
            rows = slice(b * LANE, (b + 1) * LANE)
            w = m_total * jnp.exp2((f_rows[b] + gw[:, cols]) - cross[rows, cols])
            wt[core, cols, rows] = w.T.astype(BF16)

    def wcopy(j, src, dst, dev):
        return rc(src, dst, w_send.at[j], w_recv.at[j], dev)

    low, high = pl.ds(0, HALF), pl.ds(HALF, HALF)
    copies = []
    weights(HIGH)
    copies.append(wcopy(0, wt.at[core, high], wx.at[core], other_xl))
    copies[-1].start()
    weights(LOW)
    copies.append(wcopy(1, wt.at[core, low], wt.at[core, low], other_core))
    copies[-1].start()
    copies.append(wcopy(2, wt.at[core, high], wt.at[core, high], other_core))
    copies[-1].start()
    for q in range(2):
        rc(no.at[:, :, pl.ds(q * LANE, LANE)], no.at[:, :, pl.ds(q * LANE, LANE)],
           o_send.at[q], o_recv.at[q], other_core).wait_recv()
    wcopy(1, wt.at[core, low], wt.at[1 - core, low], other_core).wait_recv()

    def mine(d, q):
        return nz[d, :, pl.ds(pl.multiple_of(q * 256 + core * LANE, LANE), LANE)]

    def theirs(d, q):
        return no[d, :, pl.ds(pl.multiple_of(q * LANE, LANE), LANE)]

    def partial(rel):
        d = (z + rel) % Z
        part[rel] = jnp.dot(
            wt[core, LOW, :], jnp.concatenate([mine(d, q) for q in (1 - xl, xl)], axis=1),
            preferred_element_type=F32,
        ) + jnp.dot(
            wt[1 - core, LOW, :], jnp.concatenate([theirs(d, q) for q in (1 - xl, xl)], axis=1),
            preferred_element_type=F32,
        )

    def partial_high(rel):
        d = (z + rel) % Z
        parth[rel] = (
            jnp.dot(wt[core, HIGH, :], mine(d, xl), preferred_element_type=F32)
            + jnp.dot(wt[1 - core, HIGH, :], theirs(d, xl), preferred_element_type=F32)
        ) + (
            jnp.dot(wx[0], nx[0, d], preferred_element_type=F32)
            + jnp.dot(wx[1], nx[1, d], preferred_element_type=F32)
        )

    def piece(k, bufs, dr, s):
        ref = bufs[1].at[dr, 4 - s] if k == 2 else bufs[0].at[dr, 4 - s, k]
        return ref.at[pl.ds(dr * LANE, LANE)] if s == 4 else ref

    def ring_copy(k, dr, s):
        ss, rs = (t_send.at[dr, 4 - s], t_recv.at[dr, 4 - s]) if k == 2 else (
            s_send.at[dr, 4 - s, k], s_recv.at[dr, 4 - s, k])
        return rc(
            piece(k, (stage, stageh), dr, s), piece(k, (land, landh), dr, s), ss, rs,
            z_dn if dr == 0 else z_up,
        )

    def own_part(k, rel, rows):
        return parth[rel, rows, :] if k == 2 else part[rel, rows, k * LANE:(k + 1) * LANE]

    def got(k, dr, s, rows):
        v = landh[dr, 4 - s, rows, :] if k == 2 else land[dr, 4 - s, k, rows, :]
        return v.astype(F32)

    def put(k, dr, s, rows, v):
        if k == 2:
            stageh[dr, 4 - s, rows, :] = v.astype(BF16)
        else:
            stage[dr, 4 - s, k, rows, :] = v.astype(BF16)

    ALL = slice(0, HALF)

    def ring_step(k, s):
        for dr in range(2):
            rel = Z - s if dr == 0 else s
            first = slice(dr * LANE, (dr + 1) * LANE)
            other = slice((1 - dr) * LANE, (2 - dr) * LANE)
            if s == 4:
                put(k, dr, s, first, own_part(k, 4, first))
            else:
                ring_copy(k, dr, s + 1).wait_recv()
                if s == 3:
                    put(k, dr, s, first, own_part(k, rel, first) + got(k, dr, 4, first))
                    put(k, dr, s, other, own_part(k, rel, other))
                else:
                    put(k, dr, s, ALL, own_part(k, rel, ALL) + got(k, dr, s + 1, ALL))
            c = ring_copy(k, dr, s)
            c.start()
            sent.append(c)

    def total(k):
        for dr in range(2):
            ring_copy(k, dr, 1).wait_recv()
        return own_part(k, 0, ALL) + (got(k, 0, 1, ALL) + got(k, 1, 1, ALL))

    partial(4)
    ring_step(0, 4)
    ring_step(1, 4)
    partial(5)
    partial(3)
    ring_step(0, 3)
    ring_step(1, 3)
    partial(6)
    partial(2)
    ring_step(0, 2)
    ring_step(1, 2)
    wcopy(0, wt.at[core, high], wx.at[core], other_xl).wait_recv()
    copies.append(wcopy(3, wx.at[core], wx.at[core], other_core))
    copies[-1].start()
    partial(7)
    partial(1)
    wcopy(2, wt.at[core, high], wt.at[1 - core, high], other_core).wait_recv()
    for c in range(2):
        for slot in range(Z):
            rc(nx.at[c, slot], nx.at[c, slot], p_send.at[0, slot], p_recv.at[c, slot], other_xl).wait_recv()
    wcopy(3, wx.at[core], wx.at[1 - core], other_core).wait_recv()
    partial_high(4)
    ring_step(2, 4)
    ring_step(0, 1)
    ring_step(1, 1)
    partial_high(5)
    partial_high(3)
    ring_step(2, 3)
    partial_high(6)
    partial_high(2)
    ring_step(2, 2)
    partial(0)
    xs[...] = total(0)
    xc = rc(xs, xr, x_send.at[0], x_recv.at[0], other_xl)
    xc.start()
    copies.append(xc)
    partial_high(7)
    partial_high(1)
    ring_step(2, 1)
    partial_high(0)
    kept = total(1)
    xc.wait_recv()
    out_ref[:, LOW] = (kept + xr[...]).T
    out_ref[:, HIGH] = total(2).T
    sent.extend(copies)

    for c in sent:
        c.wait_send()
    for it in range(ITERS):
        for buf, k, ssem, rsem in (
            (rowx, 7, r_send, r_recv), (col2, 31, c2_send, c2_recv)
        ):
            ref = buf.at[it, pl.ds(0, k)]
            rc(ref, ref, ssem.at[it], rsem.at[it], z_up).wait_send()


def per_device(n_total, m_total, noise_draw, latent_code, start_potential):
    anyspace = pl.BlockSpec(memory_space=pltpu.HBM)
    vmem = pl.BlockSpec(memory_space=pltpu.VMEM)
    width = 4096
    dma = pltpu.SemaphoreType.DMA

    def body(*refs):
        kernel(n_total, m_total, width, *refs)

    npot, lpot, out = pl.pallas_call(
        body,
        out_shape=(
            jax.ShapeDtypeStruct((4, LANE), F32),
            jax.ShapeDtypeStruct((4, LANE), F32),
            jax.ShapeDtypeStruct((LANE, BLK), F32),
        ),
        in_specs=[anyspace, anyspace, vmem],
        out_specs=(vmem, vmem, vmem),
        scratch_shapes=[
            pltpu.VMEM((8, BLK, BLK), BF16),
            pltpu.VMEM((Z, 2, 2, BLK, LANE), BF16),
            pltpu.VMEM((8, BLK, 2 * LANE), BF16),
            pltpu.VMEM((2, 2, 2, BLK // 4, BLK), BF16),
            pltpu.VMEM((BLK, BLK), F32),
            pltpu.VMEM((BLK, LANE), F32),
            pltpu.VMEM((BLK, LANE), F32),
            pltpu.VMEM((2, BLK, BLK), BF16),
            pltpu.VMEM((2, HALF, BLK), BF16),
            pltpu.VMEM((2, Z, BLK, LANE), BF16),
            pltpu.VMEM((Z, HALF, 2 * LANE), F32),
            pltpu.VMEM((Z, HALF, LANE), F32),
            pltpu.VMEM((2, 4, 2, HALF, LANE), BF16),
            pltpu.VMEM((2, 4, 2, HALF, LANE), BF16),
            pltpu.VMEM((2, 4, HALF, LANE), BF16),
            pltpu.VMEM((2, 4, HALF, LANE), BF16),
            pltpu.VMEM((HALF, LANE), F32),
            pltpu.VMEM((HALF, LANE), F32),
            pltpu.VMEM((ITERS, 8, 4, LANE), F32),
            pltpu.VMEM((ITERS, 32, 4, LANE), F32),
            dma((10,)), dma((10,)),
            dma((2, 2, 2, 2)), dma((2, 2, 2, 2)),
            dma((19,)), dma((19,)),
            dma((2,)), dma((2,)),
            dma((4,)), dma((4,)),
            dma((2, Z)), dma((2, Z)),
            dma((ITERS,)), dma((ITERS,)),
            dma((ITERS,)), dma((ITERS,)),
            dma((2, 4, 2)), dma((2, 4, 2)),
            dma((2, 4)), dma((2, 4)),
            dma((1,)), dma((1,)),
            dma((2,)),
        ],
        compiler_params=pltpu.CompilerParams(
            collective_id=0, has_side_effects=True, vmem_limit_bytes=54656 * 1024
        ),
    )(noise_draw, latent_code, start_potential.reshape(4, LANE))
    return npot.reshape(BLK), lpot.reshape(BLK), out


def solution(mesh):
    in_specs = (P("row", "col"), P("col", "row"), P("col"))
    out_specs = (P("row"), P("col"), P("row", "col"))

    def whole(noise_draw, latent_code, start_potential):
        def block(a, b, c):
            return per_device(noise_draw.shape[0], latent_code.shape[0], a, b, c)

        return jax.shard_map(
            block, mesh=mesh, in_specs=in_specs, out_specs=out_specs, check_vma=False
        )(noise_draw, latent_code, start_potential)

    return whole
```

profile of v0, /device:TPU:2, one launch (start us, length us, event | category | flops | bytes accessed | tf_op | source)
XLA Modules:
  0.0 111.1 jit_solution(1174979628793358894)
XLA Ops:
  0.6 0.0 copy-start
  0.6 0.9 copy-done
  1.5 0.0 copy-start.1
  1.5 0.7 copy-done.1
  2.2 107.1 %shard_map.58 = (f32[4,128]{1,0:T(4,128)S(1)}, f32[4,128]{1,0:T(4,128)S(1)}, f32[128,512]{1,0:T(8,128)S(1)}) custom-call(bf16[512,512]{1,0:T(8,128)(2,1)} %refs_0_.1, bf16[512,128]{1,0:T(8,128)(2,1)S(1)} %copy-done, f32[4,128]{1,0:T(4,128)S(1)} %bitcast.3), custom_call_target="tpu_custom_call" | custom-call | tf_op jit(solution)/shard_map/pallas_call | solution.py:510
  109.3 0.6 copy.9
  109.9 0.6 copy.10
  110.4 0.7 copy.11
Async XLA Ops:
  0.6 0.9 copy-start
  1.5 0.7 copy-start.1
where the time goes:
time: 111 us
  Pallas kernels  107 us (96%)
  local copies, waits for them, and re-layouts  3.44 us (3%)
    pallas_call x1, Pallas kernels, per_device(): pl.pallas_call(body, out_shape=(jax.ShapeDtypeStruct((4, LANE), F32), jax...  107 us
    unnamed x7, local copies, waits for them, and re-layouts  3.44 us

commit v1 on v0

--- a/solution.py
+++ b/solution.py
@@ -142,36 +142,52 @@
 
     own_pair = lt.at[z, core]
     own_block = lt.at[z, core, xl]
+    z_dirs = ((0, -1, z_up), (1, 1, z_dn))
+
+    def lat(d, part):
+        return lt.at[ring_z(d), core, xl if part == 0 else 1 - xl]
+
+    def lat_forward(step, part, dirs):
+        for dr, sgn, dev in dirs:
+            block = lat(sgn * step, part)
+            lwait(block, 1 + 8 * dr + 2 * (step - 1) + part)
+            if step < 3 or part == dr:
+                lsend(block, 1 + 8 * dr + 2 * step + part, dev)
+
+    def lat_share(step):
+        for dr, sgn, _ in z_dirs:
+            lsend(lt.at[ring_z(sgn * step), core], 16 + 2 * step + dr, other_core)
+
     lsend(own_block, 0, other_xl, latent_ref)
+    lsend(own_block, 1, z_up, latent_ref)
+    lsend(own_block, 9, z_dn, latent_ref)
+    sent.append(nsend(col, 0, 0, y_up, own_half(0)))
+    sent.append(nsend(col, 1, 3, y_dn, own_half(1)))
+
+    lwait(lat(0, 1), 0)
+    lsend(lat(0, 1), 2, z_up)
+    lsend(lat(0, 1), 10, z_dn)
     for p in range(2):
         relay_start(0, 0, p)
         relay_start(0, 1, p)
-    sent.append(nsend(col, 0, 0, y_up, own_half(0)))
-    sent.append(nsend(col, 1, 3, y_dn, own_half(1)))
-    lsend(own_block, 1, z_up, latent_ref)
-    lsend(own_block, 6, z_dn, latent_ref)
-
-    lwait(lt.at[z, core, 1 - xl], 0)
-    lsend(lt.at[z, core, 1 - xl], 2, z_up)
-    lsend(lt.at[z, core, 1 - xl], 7, z_dn)
+    lat_forward(1, 0, z_dirs)
     own_l.wait()
-    lsend(own_pair, 11, other_core)
+    lsend(own_pair, 17, other_core)
 
     dn, up = slot_of(ring_y(-1), 0), slot_of(ring_y(1), 0)
     nwait(dn, 0, 0)
     onward_up = nsend(dn, 0, 4, y_up)
     nwait(up, 1, 3)
     onward_dn = nsend(up, 1, 5, y_dn)
+
+    lat_forward(1, 1, z_dirs)
+    lat_share(1)
+    lat_forward(2, 0, z_dirs)
     for p in range(2):
         relay_forward(0, 0, p)
         relay_forward(0, 1, p)
-
-    for sgn, base, dev in ((-1, 1, z_up), (1, 6, z_dn)):
-        zz = ring_z(sgn)
-        lwait(lt.at[zz, core, xl], base)
-        lwait(lt.at[zz, core, 1 - xl], base + 1)
-        lsend(lt.at[zz, core], base + 2, dev)
-        lsend(lt.at[zz, core], 12 + (base == 6), other_core)
+    lat_forward(2, 1, z_dirs)
+    lat_share(2)
 
     onward_up.wait_send()
     sent.append(nsend(col, 1, 1, y_up, own_half(1)))
@@ -185,11 +201,7 @@
     relay_start(1, 1, 0)
     relay_start(1, 1, 1)
 
-    for sgn, base, dev in ((-1, 1, z_up), (1, 6, z_dn)):
-        zz = ring_z(2 * sgn)
-        lwait(lt.at[zz, core], base + 2)
-        lsend(lt.at[zz, core], base + 3, dev)
-        lsend(lt.at[zz, core], 14 + (base == 6), other_core)
+    lat_forward(3, 0, z_dirs)
 
     relay_end(0, 0)
     sent.append(nsend(flip_col, 0, 6, y_up))
@@ -198,20 +210,16 @@
     sent.append(nsend(flip_col, 1, 9, y_dn))
     sent.append(nsend(flip_col, 1, 7, y_up))
 
-    for sgn, base, dev in ((-1, 1, z_up), (1, 6, z_dn)):
-        zz = ring_z(3 * sgn)
-        lwait(lt.at[zz, core], base + 3)
-        lsend(lt.at[zz, core, int(base == 6)], base + 4, dev)
-        lsend(lt.at[zz, core], 16 + (base == 6), other_core)
-    far = ring_z(4)
-    lwait(lt.at[far, core, 0], 5)
-    lwait(lt.at[far, core, 1], 10)
-    lsend(lt.at[far, core], 18, other_core)
+    lat_forward(3, 1, z_dirs)
+    lat_share(3)
     for p in range(2):
         for path in range(2):
             relay_forward(1, path, p)
+    lwait(lat(4, 0), 7)
+    lwait(lat(4, 1), 16)
+    lsend(lt.at[ring_z(4), core], 24, other_core)
     for j, d in enumerate((0, -1, 1, -2, 2, -3, 3, 4)):
-        lwait(lt.at[ring_z(d), 1 - core], 11 + j)
+        lwait(lt.at[ring_z(d), 1 - core], 17 + j)
 
     def accumulate(slot):
         a = nz[slot]
@@ -539,7 +547,7 @@
             pltpu.VMEM((ITERS, 32, 4, LANE), F32),
             dma((10,)), dma((10,)),
             dma((2, 2, 2, 2)), dma((2, 2, 2, 2)),
-            dma((19,)), dma((19,)),
+            dma((25,)), dma((25,)),
             dma((2,)), dma((2,)),
             dma((4,)), dma((4,)),
             dma((2, Z)), dma((2, Z)),

time: 111 us -> 109 us (0.982)
  Pallas kernels: 107 us -> 105 us
    pallas_call x1, Pallas kernels: 107 us -> 105 us  [per_device(): pl.pallas_call(body, out_shape=(jax.ShapeDtypeStruct((4, LANE), F32), jax...]
where the time goes in v1:
time: 109 us
  Pallas kernels  105 us (96%)
  local copies, waits for them, and re-layouts  3.44 us (3%)
    pallas_call x1, Pallas kernels, per_device(): pl.pallas_call(body, out_shape=(jax.ShapeDtypeStruct((4, LANE), F32), jax...  105 us
    unnamed x7, local copies, waits for them, and re-layouts  3.44 us

profile of v1, /device:TPU:2, one launch (start us, length us, event | category | flops | bytes accessed | tf_op | source)
XLA Modules:
  0.0 109.0 jit_solution(12456533254585172848)
XLA Ops:
  0.6 0.0 copy-start
  0.6 0.9 copy-done
  1.5 0.0 copy-start.1
  1.5 0.7 copy-done.1
  2.2 104.9 %shard_map.58 = (f32[4,128]{1,0:T(4,128)S(1)}, f32[4,128]{1,0:T(4,128)S(1)}, f32[128,512]{1,0:T(8,128)S(1)}) custom-call(bf16[512,512]{1,0:T(8,128)(2,1)} %refs_0_.1, bf16[512,128]{1,0:T(8,128)(2,1)S(1)} %copy-done, f32[4,128]{1,0:T(4,128)S(1)} %bitcast.3), custom_call_target="tpu_custom_call" | custom-call | tf_op jit(solution)/shard_map/pallas_call | solution.py:518
  107.2 0.6 copy.9
  107.7 0.6 copy.10
  108.3 0.7 copy.11
Async XLA Ops:
  0.6 0.9 copy-start
  1.5 0.7 copy-start.1

commit v2 on v1

--- a/solution.py
+++ b/solution.py
@@ -25,7 +25,7 @@
     noise_ref, latent_ref, start_ref,
     npot_ref, lpot_ref, out_ref,
     nz, lt, no, relay, cross, nsq, lsq, wt, wx, nx, part, parth, stage, land, stageh, landh, xs, xr, rowx, col2,
-    n_send, n_recv, h_send, h_recv, l_send, l_recv, o_send, o_recv, w_send, w_recv,
+    q_send, q_recv, n_send, n_recv, h_send, h_recv, l_send, l_recv, o_send, o_recv, w_send, w_recv,
     p_send, p_recv, r_send, r_recv, c2_send, c2_recv,
     s_send, s_recv, t_send, t_recv, x_send, x_recv, loc,
 ):
@@ -73,8 +73,6 @@
     for peer in peers:
         pl.semaphore_signal(barrier, inc=1, device_id=peer, device_id_type=MESH)
     cross[...] = jnp.zeros_like(cross)
-    nsq[...] = jnp.zeros_like(nsq)
-    lsq[...] = jnp.zeros_like(lsq)
     pl.semaphore_wait(barrier, len(peers))
 
     def rc(src, dst, ssem, rsem, dev):
@@ -164,6 +162,16 @@
     sent.append(nsend(col, 0, 0, y_up, own_half(0)))
     sent.append(nsend(col, 1, 3, y_dn, own_half(1)))
 
+    own_n.wait()
+    own_l.wait()
+    for b in range(4):
+        rows = slice(b * LANE, (b + 1) * LANE)
+        n2 = jnp.square(nz[col, rows, :].astype(F32))
+        n2 = (n2[:, 0:128] + n2[:, 128:256]) + (n2[:, 256:384] + n2[:, 384:512])
+        nsq[col, b:b + 1, :] = jnp.sum(n2.T, axis=0, keepdims=True)
+        l2 = jnp.square(lt[z, core, xl, rows, :].astype(F32))
+        lsq[row, b:b + 1, :] = jnp.sum(l2.T, axis=0, keepdims=True)
+
     lwait(lat(0, 1), 0)
     lsend(lat(0, 1), 2, z_up)
     lsend(lat(0, 1), 10, z_dn)
@@ -171,7 +179,6 @@
         relay_start(0, 0, p)
         relay_start(0, 1, p)
     lat_forward(1, 0, z_dirs)
-    own_l.wait()
     lsend(own_pair, 17, other_core)
 
     dn, up = slot_of(ring_y(-1), 0), slot_of(ring_y(1), 0)
@@ -182,6 +189,10 @@
 
     lat_forward(1, 1, z_dirs)
     lat_share(1)
+    for peer in col_peers:
+        rc(nsq.at[col], nsq.at[col], q_send.at[0], q_recv.at[0], peer).start()
+    for peer in row_peers:
+        rc(lsq.at[row], lsq.at[row], q_send.at[1], q_recv.at[1], peer).start()
     lat_forward(2, 0, z_dirs)
     for p in range(2):
         relay_forward(0, 0, p)
@@ -225,17 +236,12 @@
         a = nz[slot]
         b = jnp.concatenate([lt[slot, 0, 0], lt[slot, 1, 0], lt[slot, 0, 1], lt[slot, 1, 1]], axis=1)
         cross[...] += lax.dot_general(a, b, (((1,), (1,)), ((), ())), preferred_element_type=F32)
-        a2 = jnp.square(a.astype(F32))
-        nsq[...] += (a2[:, 0:128] + a2[:, 128:256]) + (a2[:, 256:384] + a2[:, 384:512])
-        b2 = jnp.square(b.astype(F32))
-        lsq[...] += (b2[:, 0:128] + b2[:, 128:256]) + (b2[:, 256:384] + b2[:, 384:512])
 
     def wait_rest(s):
         dn, up = slot_of(ring_y(-1), s), slot_of(ring_y(1), s)
         nwait(dn, 1, 6 * s + 1)
         nwait(up, 0, 6 * s + 2)
 
-    own_n.wait()
     wait_rest(0)
 
     def set0(k, carry):
@@ -268,9 +274,6 @@
         == lax.broadcasted_iota(jnp.int32, (LANE, LANE), 1)
     )
 
-    def to_lanes(v):
-        return jnp.sum(jnp.where(eye, v, 0.0), axis=0, keepdims=True)
-
     def to_rows(v):
         return jnp.sum(jnp.where(eye, v, 0.0), axis=1, keepdims=True)
 
@@ -278,14 +281,13 @@
         return jnp.concatenate([v[q:q + 1, :] for q in range(4)], axis=1)
 
     scale = LOG2E / (width * EPS)
-    lq = jnp.concatenate(
-        [to_lanes(jnp.sum(lsq[q * LANE:(q + 1) * LANE, :], axis=1, keepdims=True)) for q in range(4)],
-        axis=1,
-    )
+    rc(nsq.at[pl.ds(0, 7)], nsq.at[pl.ds(0, 7)], q_send.at[0], q_recv.at[0], z_up).wait_recv()
+    rc(lsq.at[pl.ds(0, 31)], lsq.at[pl.ds(0, 31)], q_send.at[1], q_recv.at[1], z_up).wait_recv()
+    nq = jnp.sum(nsq[...], axis=0)
+    lq = wide(jnp.sum(lsq[...], axis=0))
     for b in range(4):
         rows = slice(b * LANE, (b + 1) * LANE)
-        nq = jnp.sum(nsq[rows, :], axis=1, keepdims=True)
-        cross[rows, :] = (nq + lq - 2.0 * cross[rows, :]) * scale
+        cross[rows, :] = (to_rows(nq[b:b + 1, :]) + lq - 2.0 * cross[rows, :]) * scale
 
     def merge(parts):
         best = jnp.max(parts, axis=0)
@@ -361,18 +363,14 @@
 
     low, high = pl.ds(0, HALF), pl.ds(HALF, HALF)
     copies = []
+    weights(LOW)
+    copies.append(wcopy(1, wt.at[core, low], wt.at[core, low], other_core))
+    copies[-1].start()
     weights(HIGH)
     copies.append(wcopy(0, wt.at[core, high], wx.at[core], other_xl))
     copies[-1].start()
-    weights(LOW)
-    copies.append(wcopy(1, wt.at[core, low], wt.at[core, low], other_core))
-    copies[-1].start()
     copies.append(wcopy(2, wt.at[core, high], wt.at[core, high], other_core))
     copies[-1].start()
-    for q in range(2):
-        rc(no.at[:, :, pl.ds(q * LANE, LANE)], no.at[:, :, pl.ds(q * LANE, LANE)],
-           o_send.at[q], o_recv.at[q], other_core).wait_recv()
-    wcopy(1, wt.at[core, low], wt.at[1 - core, low], other_core).wait_recv()
 
     def mine(d, q):
         return nz[d, :, pl.ds(pl.multiple_of(q * 256 + core * LANE, LANE), LANE)]
@@ -380,15 +378,23 @@
     def theirs(d, q):
         return no[d, :, pl.ds(pl.multiple_of(q * LANE, LANE), LANE)]
 
-    def partial(rel):
+    def partial_own(rel):
         d = (z + rel) % Z
         part[rel] = jnp.dot(
             wt[core, LOW, :], jnp.concatenate([mine(d, q) for q in (1 - xl, xl)], axis=1),
             preferred_element_type=F32,
-        ) + jnp.dot(
+        )
+
+    def partial_other(rel):
+        d = (z + rel) % Z
+        part[rel] += jnp.dot(
             wt[1 - core, LOW, :], jnp.concatenate([theirs(d, q) for q in (1 - xl, xl)], axis=1),
             preferred_element_type=F32,
         )
+
+    def partial(rel):
+        partial_own(rel)
+        partial_other(rel)
 
     def partial_high(rel):
         d = (z + rel) % Z
@@ -450,11 +456,17 @@
             ring_copy(k, dr, 1).wait_recv()
         return own_part(k, 0, ALL) + (got(k, 0, 1, ALL) + got(k, 1, 1, ALL))
 
-    partial(4)
+    for rel in (4, 5, 3):
+        partial_own(rel)
+    for q in range(2):
+        rc(no.at[:, :, pl.ds(q * LANE, LANE)], no.at[:, :, pl.ds(q * LANE, LANE)],
+           o_send.at[q], o_recv.at[q], other_core).wait_recv()
+    wcopy(1, wt.at[core, low], wt.at[1 - core, low], other_core).wait_recv()
+    partial_other(4)
     ring_step(0, 4)
     ring_step(1, 4)
-    partial(5)
-    partial(3)
+    partial_other(5)
+    partial_other(3)
     ring_step(0, 3)
     ring_step(1, 3)
     partial(6)
@@ -496,6 +508,9 @@
     out_ref[:, HIGH] = total(2).T
     sent.extend(copies)
 
+    for j, (buf, k) in enumerate(((nsq, 7), (lsq, 31))):
+        ref = buf.at[pl.ds(0, k)]
+        rc(ref, ref, q_send.at[j], q_recv.at[j], z_up).wait_send()
     for c in sent:
         c.wait_send()
     for it in range(ITERS):
@@ -530,8 +545,8 @@
             pltpu.VMEM((8, BLK, 2 * LANE), BF16),
             pltpu.VMEM((2, 2, 2, BLK // 4, BLK), BF16),
             pltpu.VMEM((BLK, BLK), F32),
-            pltpu.VMEM((BLK, LANE), F32),
-            pltpu.VMEM((BLK, LANE), F32),
+            pltpu.VMEM((8, 4, LANE), F32),
+            pltpu.VMEM((32, 4, LANE), F32),
             pltpu.VMEM((2, BLK, BLK), BF16),
             pltpu.VMEM((2, HALF, BLK), BF16),
             pltpu.VMEM((2, Z, BLK, LANE), BF16),
@@ -545,6 +560,7 @@
             pltpu.VMEM((HALF, LANE), F32),
             pltpu.VMEM((ITERS, 8, 4, LANE), F32),
             pltpu.VMEM((ITERS, 32, 4, LANE), F32),
+            dma((2,)), dma((2,)),
             dma((10,)), dma((10,)),
             dma((2, 2, 2, 2)), dma((2, 2, 2, 2)),
             dma((25,)), dma((25,)),

time: 109 us -> 109 us (level)
  no operation moved by 1% of the time
where the time goes in v2:
time: 109 us
  Pallas kernels  105 us (96%)
  local copies, waits for them, and re-layouts  3.44 us (3%)
    pallas_call x1, Pallas kernels, per_device(): pl.pallas_call(body, out_shape=(jax.ShapeDtypeStruct((4, LANE), F32), jax...  105 us
    unnamed x7, local copies, waits for them, and re-layouts  3.44 us

profile of v2, /device:TPU:2, one launch (start us, length us, event | category | flops | bytes accessed | tf_op | source)
XLA Modules:
  0.0 109.3 jit_solution(14198453326057640936)
XLA Ops:
  0.6 0.0 copy-start
  0.6 0.9 copy-done
  1.5 0.0 copy-start.1
  1.5 0.7 copy-done.1
  2.2 105.2 %shard_map.58 = (f32[4,128]{1,0:T(4,128)S(1)}, f32[4,128]{1,0:T(4,128)S(1)}, f32[128,512]{1,0:T(8,128)S(1)}) custom-call(bf16[512,512]{1,0:T(8,128)(2,1)} %refs_0_.1, bf16[512,128]{1,0:T(8,128)(2,1)S(1)} %copy-done, f32[4,128]{1,0:T(4,128)S(1)} %bitcast.3), custom_call_target="tpu_custom_call" | custom-call | tf_op jit(solution)/shard_map/pallas_call | solution.py:533
  107.5 0.6 copy.9
  108.1 0.6 copy.10
  108.6 0.7 copy.11
Async XLA Ops:
  0.6 0.9 copy-start
  1.5 0.7 copy-start.1

commit v3 on v2

--- a/solution.py
+++ b/solution.py
@@ -18,13 +18,15 @@
 LANE = 128
 BLK = 512
 HALF = BLK // 2
+SPLIT = 384
+REST = BLK - SPLIT
 
 
 def kernel(
     n_total, m_total, width,
     noise_ref, latent_ref, start_ref,
     npot_ref, lpot_ref, out_ref,
-    nz, lt, no, relay, cross, nsq, lsq, wt, wx, nx, part, parth, stage, land, stageh, landh, xs, xr, rowx, col2,
+    nz, lt, no, cross, nsq, lsq, wt, wx, nx, part, parth, stage, land, stageh, landh, xs, xr, rowx, col2,
     q_send, q_recv, n_send, n_recv, h_send, h_recv, l_send, l_recv, o_send, o_recv, w_send, w_recv,
     p_send, p_recv, r_send, r_recv, c2_send, c2_recv,
     s_send, s_recv, t_send, t_recv, x_send, x_recv, loc,
@@ -47,7 +49,7 @@
     other_core = (row + 1 - 2 * core, col)
     other_xl = (row + 2 - 4 * xl, col)
     flip_col = col + 1 - 2 * xh
-    diagonal = (row + 2 - 4 * xl, flip_col)
+    other_xh = (row, flip_col)
     z_up = (ring_z(1) * 4 + quad, col)
     z_dn = (ring_z(-1) * 4 + quad, col)
     y_up = (row, ring_y(1) * 2 + xh)
@@ -84,6 +86,7 @@
     def nsl(slot, h):
         return nz.at[slot, pl.ds(h * HALF, HALF), :]
 
+    QUART = HALF // 2
     sent = []
 
     def nsend(slot, h, idx, dev, src=None):
@@ -106,37 +109,21 @@
     def lwait(ref, idx):
         rc(ref, ref, l_send.at[idx], l_recv.at[idx], z_up).wait_recv()
 
-    QUART = HALF // 2
-
     def slot_of(yy, s):
         return yy * 2 + (xh if s == 0 else 1 - xh)
 
-    def quarter(slot, path, p):
-        return nz.at[slot, pl.ds(path * HALF + p * QUART, QUART), :]
-
-    def relay_start(t, path, p):
-        if t == 0:
-            ref = noise_ref.at[pl.ds(path * HALF + p * QUART, QUART), :]
-        else:
-            ref = quarter(slot_of(ring_y(2), 0), path, p)
-        c = rc(ref, relay.at[t, path, p], h_send.at[0, t, path, p], h_recv.at[0, t, path, p],
-               other_xl if path == 0 else diagonal)
+    def xh_copy(t, h, src, slot):
+        return rc(src, nsl(slot, h), h_send.at[t, h], h_recv.at[t, h], other_xh)
+
+    def xh_send(t, h):
+        far0 = slot_of(ring_y(2), 0)
+        c = xh_copy(t, h, own_half(h), col) if t == 0 else xh_copy(t, h, nsl(far0, h), far0)
         c.start()
         sent.append(c)
 
-    def relay_forward(t, path, p):
-        ref = quarter(slot_of(ring_y(2 * t), path), path, p)
-        dev = diagonal if path == 0 else other_xl
-        buf = relay.at[t, path, p]
-        rc(buf, buf, h_send.at[0, t, path, p], h_recv.at[0, t, path, p], dev).wait_recv()
-        c = rc(buf, ref, h_send.at[1, t, path, p], h_recv.at[1, t, path, p], dev)
-        c.start()
-        sent.append(c)
-
-    def relay_end(t, path):
-        for p in range(2):
-            ref = quarter(slot_of(ring_y(2 * t), 1), path, p)
-            rc(ref, ref, h_send.at[1, t, path, p], h_recv.at[1, t, path, p], diagonal).wait_recv()
+    def xh_wait(t, h):
+        slot = flip_col if t == 0 else slot_of(ring_y(2), 1)
+        xh_copy(t, h, nsl(slot, h), slot).wait_recv()
 
     own_pair = lt.at[z, core]
     own_block = lt.at[z, core, xl]
@@ -159,8 +146,10 @@
     lsend(own_block, 0, other_xl, latent_ref)
     lsend(own_block, 1, z_up, latent_ref)
     lsend(own_block, 9, z_dn, latent_ref)
-    sent.append(nsend(col, 0, 0, y_up, own_half(0)))
-    sent.append(nsend(col, 1, 3, y_dn, own_half(1)))
+    first_up = nsend(col, 0, 0, y_up, own_half(0))
+    first_dn = nsend(col, 1, 3, y_dn, own_half(1))
+    xh_send(0, 0)
+    xh_send(0, 1)
 
     own_n.wait()
     own_l.wait()
@@ -175,11 +164,19 @@
     lwait(lat(0, 1), 0)
     lsend(lat(0, 1), 2, z_up)
     lsend(lat(0, 1), 10, z_dn)
-    for p in range(2):
-        relay_start(0, 0, p)
-        relay_start(0, 1, p)
     lat_forward(1, 0, z_dirs)
     lsend(own_pair, 17, other_core)
+
+    def own_quarter(h, p, idx, dev):
+        at = pl.ds(h * HALF + p * QUART, QUART)
+        c = rc(noise_ref.at[at, :], nz.at[col, at, :], n_send.at[idx], n_recv.at[idx], dev)
+        c.start()
+        sent.append(c)
+
+    first_up.wait_send()
+    own_quarter(1, 0, 1, y_up)
+    first_dn.wait_send()
+    own_quarter(0, 0, 2, y_dn)
 
     dn, up = slot_of(ring_y(-1), 0), slot_of(ring_y(1), 0)
     nwait(dn, 0, 0)
@@ -194,38 +191,30 @@
     for peer in row_peers:
         rc(lsq.at[row], lsq.at[row], q_send.at[1], q_recv.at[1], peer).start()
     lat_forward(2, 0, z_dirs)
-    for p in range(2):
-        relay_forward(0, 0, p)
-        relay_forward(0, 1, p)
     lat_forward(2, 1, z_dirs)
     lat_share(2)
 
     onward_up.wait_send()
-    sent.append(nsend(col, 1, 1, y_up, own_half(1)))
+    own_quarter(1, 1, 10, y_up)
     onward_dn.wait_send()
-    sent.append(nsend(col, 0, 2, y_dn, own_half(0)))
+    own_quarter(0, 1, 11, y_dn)
 
     nwait(slot_of(ring_y(2), 0), 0, 4)
-    relay_start(1, 0, 0)
-    relay_start(1, 0, 1)
+    xh_send(1, 0)
     nwait(slot_of(ring_y(2), 0), 1, 5)
-    relay_start(1, 1, 0)
-    relay_start(1, 1, 1)
+    xh_send(1, 1)
 
     lat_forward(3, 0, z_dirs)
 
-    relay_end(0, 0)
+    xh_wait(0, 0)
     sent.append(nsend(flip_col, 0, 6, y_up))
     sent.append(nsend(flip_col, 0, 8, y_dn))
-    relay_end(0, 1)
+    xh_wait(0, 1)
     sent.append(nsend(flip_col, 1, 9, y_dn))
     sent.append(nsend(flip_col, 1, 7, y_up))
 
     lat_forward(3, 1, z_dirs)
     lat_share(3)
-    for p in range(2):
-        for path in range(2):
-            relay_forward(1, path, p)
     lwait(lat(4, 0), 7)
     lwait(lat(4, 1), 16)
     lsend(lt.at[ring_z(4), core], 24, other_core)
@@ -237,12 +226,11 @@
         b = jnp.concatenate([lt[slot, 0, 0], lt[slot, 1, 0], lt[slot, 0, 1], lt[slot, 1, 1]], axis=1)
         cross[...] += lax.dot_general(a, b, (((1,), (1,)), ((), ())), preferred_element_type=F32)
 
-    def wait_rest(s):
-        dn, up = slot_of(ring_y(-1), s), slot_of(ring_y(1), s)
-        nwait(dn, 1, 6 * s + 1)
-        nwait(up, 0, 6 * s + 2)
-
-    wait_rest(0)
+    dn, up = slot_of(ring_y(-1), 0), slot_of(ring_y(1), 0)
+    for slot, h, idxs in ((dn, 1, (1, 10)), (up, 0, (2, 11))):
+        for p in range(2):
+            ref = nz.at[slot, pl.ds(h * HALF + p * QUART, QUART), :]
+            rc(ref, ref, n_send.at[idxs[p]], n_recv.at[idxs[p]], y_up).wait_recv()
 
     def set0(k, carry):
         accumulate(((y + k) % Y) * 2 + xh)
@@ -250,13 +238,14 @@
 
     lax.fori_loop(0, Y, set0, 0)
     accumulate(flip_col)
-    relay_end(1, 0)
-    relay_end(1, 1)
+    xh_wait(1, 0)
+    xh_wait(1, 1)
     accumulate(slot_of(ring_y(2), 1))
     dn, up = slot_of(ring_y(-1), 1), slot_of(ring_y(1), 1)
     nwait(dn, 0, 6)
     nwait(up, 1, 9)
-    wait_rest(1)
+    nwait(dn, 1, 7)
+    nwait(up, 0, 8)
     accumulate(dn)
     accumulate(up)
 
@@ -349,7 +338,7 @@
     npot_ref[...] = f * (EPS / LOG2E)
     lpot_ref[...] = g * (EPS / LOG2E)
 
-    LOW, HIGH = slice(0, HALF), slice(HALF, BLK)
+    LOW, HIGH = slice(0, SPLIT), slice(SPLIT, BLK)
     gw = wide(g)
 
     def weights(cols):
@@ -358,16 +347,17 @@
             w = m_total * jnp.exp2((f_rows[b] + gw[:, cols]) - cross[rows, cols])
             wt[core, cols, rows] = w.T.astype(BF16)
 
-    def wcopy(j, src, dst, dev):
-        return rc(src, dst, w_send.at[j], w_recv.at[j], dev)
-
-    low, high = pl.ds(0, HALF), pl.ds(HALF, HALF)
+    def wcopy(j, src, dst, dev, r=None):
+        return rc(src, dst, w_send.at[j], w_recv.at[j if r is None else 3 * r], dev)
+
+    low, high = pl.ds(0, SPLIT), pl.ds(SPLIT, REST)
     copies = []
+    weights(HIGH)
+    for k in range(2):
+        copies.append(wcopy(3 * k, wt.at[core, high], wx.at[core], (across + k, col), core))
+        copies[-1].start()
     weights(LOW)
     copies.append(wcopy(1, wt.at[core, low], wt.at[core, low], other_core))
-    copies[-1].start()
-    weights(HIGH)
-    copies.append(wcopy(0, wt.at[core, high], wx.at[core], other_xl))
     copies[-1].start()
     copies.append(wcopy(2, wt.at[core, high], wt.at[core, high], other_core))
     copies[-1].start()
@@ -406,9 +396,13 @@
             + jnp.dot(wx[1], nx[1, d], preferred_element_type=F32)
         )
 
+    def size(k):
+        return REST if k == 2 else SPLIT
+
     def piece(k, bufs, dr, s):
         ref = bufs[1].at[dr, 4 - s] if k == 2 else bufs[0].at[dr, 4 - s, k]
-        return ref.at[pl.ds(dr * LANE, LANE)] if s == 4 else ref
+        h = size(k) // 2
+        return ref.at[pl.ds(dr * h, h)] if s == 4 else ref
 
     def ring_copy(k, dr, s):
         ss, rs = (t_send.at[dr, 4 - s], t_recv.at[dr, 4 - s]) if k == 2 else (
@@ -431,13 +425,13 @@
         else:
             stage[dr, 4 - s, k, rows, :] = v.astype(BF16)
 
-    ALL = slice(0, HALF)
-
     def ring_step(k, s):
+        h = size(k) // 2
+        both = slice(0, 2 * h)
         for dr in range(2):
             rel = Z - s if dr == 0 else s
-            first = slice(dr * LANE, (dr + 1) * LANE)
-            other = slice((1 - dr) * LANE, (2 - dr) * LANE)
+            first = slice(dr * h, (dr + 1) * h)
+            other = slice((1 - dr) * h, (2 - dr) * h)
             if s == 4:
                 put(k, dr, s, first, own_part(k, 4, first))
             else:
@@ -446,15 +440,16 @@
                     put(k, dr, s, first, own_part(k, rel, first) + got(k, dr, 4, first))
                     put(k, dr, s, other, own_part(k, rel, other))
                 else:
-                    put(k, dr, s, ALL, own_part(k, rel, ALL) + got(k, dr, s + 1, ALL))
+                    put(k, dr, s, both, own_part(k, rel, both) + got(k, dr, s + 1, both))
             c = ring_copy(k, dr, s)
             c.start()
             sent.append(c)
 
     def total(k):
+        both = slice(0, size(k))
         for dr in range(2):
             ring_copy(k, dr, 1).wait_recv()
-        return own_part(k, 0, ALL) + (got(k, 0, 1, ALL) + got(k, 1, 1, ALL))
+        return own_part(k, 0, both) + (got(k, 0, 1, both) + got(k, 1, 1, both))
 
     for rel in (4, 5, 3):
         partial_own(rel)
@@ -467,45 +462,41 @@
     ring_step(1, 4)
     partial_other(5)
     partial_other(3)
-    ring_step(0, 3)
-    ring_step(1, 3)
-    partial(6)
-    partial(2)
-    ring_step(0, 2)
-    ring_step(1, 2)
-    wcopy(0, wt.at[core, high], wx.at[core], other_xl).wait_recv()
-    copies.append(wcopy(3, wx.at[core], wx.at[core], other_core))
-    copies[-1].start()
-    partial(7)
-    partial(1)
     wcopy(2, wt.at[core, high], wt.at[1 - core, high], other_core).wait_recv()
     for c in range(2):
         for slot in range(Z):
             rc(nx.at[c, slot], nx.at[c, slot], p_send.at[0, slot], p_recv.at[c, slot], other_xl).wait_recv()
-    wcopy(3, wx.at[core], wx.at[1 - core], other_core).wait_recv()
+    ring_step(0, 3)
+    ring_step(1, 3)
+    for c in range(2):
+        wcopy(0, wt.at[core, high], wx.at[c], other_xl, c).wait_recv()
     partial_high(4)
     ring_step(2, 4)
+    for rel in (6, 2):
+        partial(rel)
+    for rel in (5, 3):
+        partial_high(rel)
+    ring_step(0, 2)
+    ring_step(1, 2)
+    ring_step(2, 3)
+    for rel in (7, 1, 0):
+        partial(rel)
+    for rel in (6, 2):
+        partial_high(rel)
     ring_step(0, 1)
     ring_step(1, 1)
-    partial_high(5)
-    partial_high(3)
-    ring_step(2, 3)
-    partial_high(6)
-    partial_high(2)
     ring_step(2, 2)
-    partial(0)
+    for rel in (7, 1, 0):
+        partial_high(rel)
     xs[...] = total(0)
     xc = rc(xs, xr, x_send.at[0], x_recv.at[0], other_xl)
     xc.start()
     copies.append(xc)
-    partial_high(7)
-    partial_high(1)
     ring_step(2, 1)
-    partial_high(0)
     kept = total(1)
+    out_ref[:, HIGH] = total(2).T
     xc.wait_recv()
     out_ref[:, LOW] = (kept + xr[...]).T
-    out_ref[:, HIGH] = total(2).T
     sent.extend(copies)
 
     for j, (buf, k) in enumerate(((nsq, 7), (lsq, 31))):
@@ -543,26 +534,25 @@
             pltpu.VMEM((8, BLK, BLK), BF16),
             pltpu.VMEM((Z, 2, 2, BLK, LANE), BF16),
             pltpu.VMEM((8, BLK, 2 * LANE), BF16),
-            pltpu.VMEM((2, 2, 2, BLK // 4, BLK), BF16),
             pltpu.VMEM((BLK, BLK), F32),
             pltpu.VMEM((8, 4, LANE), F32),
             pltpu.VMEM((32, 4, LANE), F32),
             pltpu.VMEM((2, BLK, BLK), BF16),
-            pltpu.VMEM((2, HALF, BLK), BF16),
+            pltpu.VMEM((2, REST, BLK), BF16),
             pltpu.VMEM((2, Z, BLK, LANE), BF16),
-            pltpu.VMEM((Z, HALF, 2 * LANE), F32),
-            pltpu.VMEM((Z, HALF, LANE), F32),
-            pltpu.VMEM((2, 4, 2, HALF, LANE), BF16),
-            pltpu.VMEM((2, 4, 2, HALF, LANE), BF16),
-            pltpu.VMEM((2, 4, HALF, LANE), BF16),
-            pltpu.VMEM((2, 4, HALF, LANE), BF16),
-            pltpu.VMEM((HALF, LANE), F32),
-            pltpu.VMEM((HALF, LANE), F32),
+            pltpu.VMEM((Z, SPLIT, 2 * LANE), F32),
+            pltpu.VMEM((Z, REST, LANE), F32),
+            pltpu.VMEM((2, 4, 2, SPLIT, LANE), BF16),
+            pltpu.VMEM((2, 4, 2, SPLIT, LANE), BF16),
+            pltpu.VMEM((2, 4, REST, LANE), BF16),
+            pltpu.VMEM((2, 4, REST, LANE), BF16),
+            pltpu.VMEM((SPLIT, LANE), F32),
+            pltpu.VMEM((SPLIT, LANE), F32),
             pltpu.VMEM((ITERS, 8, 4, LANE), F32),
             pltpu.VMEM((ITERS, 32, 4, LANE), F32),
             dma((2,)), dma((2,)),
-            dma((10,)), dma((10,)),
-            dma((2, 2, 2, 2)), dma((2, 2, 2, 2)),
+            dma((12,)), dma((12,)),
+            dma((2, 2)), dma((2, 2)),
             dma((25,)), dma((25,)),
             dma((2,)), dma((2,)),
             dma((4,)), dma((4,)),

time: 109 us -> 107 us (0.982)
  Pallas kernels: 105 us -> 102 us
    pallas_call x1, Pallas kernels: 105 us -> 102 us  [per_device(): pl.pallas_call(body, out_shape=(jax.ShapeDtypeStruct((4, LANE), F32), jax...]
where the time goes in v3:
time: 107 us; the launch traced here: 106 us
  Pallas kernels  102 us (95%)
  local copies, waits for them, and re-layouts  3.44 us (3%)
    pallas_call x1, Pallas kernels, per_device(): pl.pallas_call(body, out_shape=(jax.ShapeDtypeStruct((4, LANE), F32), jax...  102 us
    unnamed x7, local copies, waits for them, and re-layouts  3.44 us

profile of v3, /device:TPU:2, one launch (start us, length us, event | category | flops | bytes accessed | tf_op | source)
XLA Modules:
  0.0 106.5 jit_solution(17643887595856414140)
XLA Ops:
  0.6 0.0 copy-start
  0.6 0.9 copy-done
  1.5 0.0 copy-start.1
  1.5 0.7 copy-done.1
  2.2 102.4 %shard_map.58 = (f32[4,128]{1,0:T(4,128)S(1)}, f32[4,128]{1,0:T(4,128)S(1)}, f32[128,512]{1,0:T(8,128)S(1)}) custom-call(bf16[512,512]{1,0:T(8,128)(2,1)} %refs_0_.1, bf16[512,128]{1,0:T(8,128)(2,1)S(1)} %copy-done, f32[4,128]{1,0:T(4,128)S(1)} %bitcast.3), custom_call_target="tpu_custom_call" | custom-call | tf_op jit(solution)/shard_map/pallas_call | solution.py:524
  104.6 0.6 copy.9
  105.2 0.6 copy.10
  105.8 0.7 copy.11
Async XLA Ops:
  0.6 0.9 copy-start
  1.5 0.7 copy-start.1

commit v4 on v3

--- a/solution.py
+++ b/solution.py
@@ -143,11 +143,14 @@
         for dr, sgn, _ in z_dirs:
             lsend(lt.at[ring_z(sgn * step), core], 16 + 2 * step + dr, other_core)
 
-    lsend(own_block, 0, other_xl, latent_ref)
+    lat_x = rc(latent_ref, own_block, l_send.at[0], l_recv.at[0], other_xl)
+    lat_x.start()
     lsend(own_block, 1, z_up, latent_ref)
     lsend(own_block, 9, z_dn, latent_ref)
     first_up = nsend(col, 0, 0, y_up, own_half(0))
     first_dn = nsend(col, 1, 3, y_dn, own_half(1))
+
+    lat_x.wait_send()
     xh_send(0, 0)
     xh_send(0, 1)
 
@@ -300,7 +303,7 @@
         for peer in peers:
             rc(buf.at[mine], buf.at[mine], ssem, rsem, peer).start()
         step = next(steps)
-        for piece_at in range(step * 8 // 6, (step + 1) * 8 // 6):
+        for piece_at in range(*((0, 2), (2, 4), (4, 6), (6, 7), (7, 8), (8, 8))[step]):
             lend(piece_at)
         k = len(peers)
         rc(buf.at[pl.ds(0, k)], buf.at[pl.ds(0, k)], ssem, rsem, peers[0]).wait_recv()
@@ -425,6 +428,8 @@
         else:
             stage[dr, 4 - s, k, rows, :] = v.astype(BF16)
 
+    leaving = {}
+
     def ring_step(k, s):
         h = size(k) // 2
         both = slice(0, 2 * h)
@@ -441,9 +446,10 @@
                     put(k, dr, s, other, own_part(k, rel, other))
                 else:
                     put(k, dr, s, both, own_part(k, rel, both) + got(k, dr, s + 1, both))
-            c = ring_copy(k, dr, s)
-            c.start()
-            sent.append(c)
+            if dr in leaving:
+                leaving[dr].wait_send()
+            leaving[dr] = ring_copy(k, dr, s)
+            leaving[dr].start()
 
     def total(k):
         both = slice(0, size(k))
@@ -459,45 +465,47 @@
     wcopy(1, wt.at[core, low], wt.at[1 - core, low], other_core).wait_recv()
     partial_other(4)
     ring_step(0, 4)
-    ring_step(1, 4)
     partial_other(5)
     partial_other(3)
+    ring_step(1, 4)
     wcopy(2, wt.at[core, high], wt.at[1 - core, high], other_core).wait_recv()
     for c in range(2):
         for slot in range(Z):
             rc(nx.at[c, slot], nx.at[c, slot], p_send.at[0, slot], p_recv.at[c, slot], other_xl).wait_recv()
     ring_step(0, 3)
-    ring_step(1, 3)
     for c in range(2):
         wcopy(0, wt.at[core, high], wx.at[c], other_xl, c).wait_recv()
     partial_high(4)
+    ring_step(1, 3)
+    partial(6)
+    partial(2)
     ring_step(2, 4)
-    for rel in (6, 2):
-        partial(rel)
-    for rel in (5, 3):
-        partial_high(rel)
     ring_step(0, 2)
+    partial_high(5)
+    partial_high(3)
     ring_step(1, 2)
+    partial(7)
+    partial(1)
     ring_step(2, 3)
-    for rel in (7, 1, 0):
-        partial(rel)
-    for rel in (6, 2):
-        partial_high(rel)
     ring_step(0, 1)
+    partial(0)
+    partial_high(6)
+    partial_high(2)
     ring_step(1, 1)
     ring_step(2, 2)
-    for rel in (7, 1, 0):
-        partial_high(rel)
     xs[...] = total(0)
     xc = rc(xs, xr, x_send.at[0], x_recv.at[0], other_xl)
     xc.start()
     copies.append(xc)
+    for rel in (7, 1, 0):
+        partial_high(rel)
     ring_step(2, 1)
     kept = total(1)
     out_ref[:, HIGH] = total(2).T
     xc.wait_recv()
     out_ref[:, LOW] = (kept + xr[...]).T
     sent.extend(copies)
+    sent.extend(leaving.values())
 
     for j, (buf, k) in enumerate(((nsq, 7), (lsq, 31))):
         ref = buf.at[pl.ds(0, k)]

time: 107 us -> 113 us (1.056)
  Pallas kernels: 102 us -> 108 us
    pallas_call x1, Pallas kernels: 102 us -> 108 us  [per_device(): pl.pallas_call(body, out_shape=(jax.ShapeDtypeStruct((4, LANE), F32), jax...]
where the time goes in v4:
time: 113 us; the launch traced here: 112 us
  Pallas kernels  108 us (96%)
  local copies, waits for them, and re-layouts  3.44 us (3%)
    pallas_call x1, Pallas kernels, per_device(): pl.pallas_call(body, out_shape=(jax.ShapeDtypeStruct((4, LANE), F32), jax...  108 us
    unnamed x7, local copies, waits for them, and re-layouts  3.44 us

profile of v4, /device:TPU:2, one launch (start us, length us, event | category | flops | bytes accessed | tf_op | source)
XLA Modules:
  0.0 112.4 jit_solution(8238555050085812098)
XLA Ops:
  0.6 0.0 copy-start
  0.6 0.9 copy-done
  1.5 0.0 copy-start.1
  1.5 0.7 copy-done.1
  2.2 108.3 %shard_map.58 = (f32[4,128]{1,0:T(4,128)S(1)}, f32[4,128]{1,0:T(4,128)S(1)}, f32[128,512]{1,0:T(8,128)S(1)}) custom-call(bf16[512,512]{1,0:T(8,128)(2,1)} %refs_0_.1, bf16[512,128]{1,0:T(8,128)(2,1)S(1)} %copy-done, f32[4,128]{1,0:T(4,128)S(1)} %bitcast.3), custom_call_target="tpu_custom_call" | custom-call | tf_op jit(solution)/shard_map/pallas_call | solution.py:532
  110.5 0.6 copy.9
  111.1 0.6 copy.10
  111.7 0.7 copy.11
Async XLA Ops:
  0.6 0.9 copy-start
  1.5 0.7 copy-start.1

commit v5 on v4

--- a/solution.py
+++ b/solution.py
@@ -150,7 +150,7 @@
     first_up = nsend(col, 0, 0, y_up, own_half(0))
     first_dn = nsend(col, 1, 3, y_dn, own_half(1))
 
-    lat_x.wait_send()
+    sent.append(lat_x)
     xh_send(0, 0)
     xh_send(0, 1)
 
@@ -428,8 +428,6 @@
         else:
             stage[dr, 4 - s, k, rows, :] = v.astype(BF16)
 
-    leaving = {}
-
     def ring_step(k, s):
         h = size(k) // 2
         both = slice(0, 2 * h)
@@ -446,10 +444,9 @@
                     put(k, dr, s, other, own_part(k, rel, other))
                 else:
                     put(k, dr, s, both, own_part(k, rel, both) + got(k, dr, s + 1, both))
-            if dr in leaving:
-                leaving[dr].wait_send()
-            leaving[dr] = ring_copy(k, dr, s)
-            leaving[dr].start()
+            c = ring_copy(k, dr, s)
+            c.start()
+            sent.append(c)
 
     def total(k):
         both = slice(0, size(k))
@@ -505,7 +502,6 @@
     xc.wait_recv()
     out_ref[:, LOW] = (kept + xr[...]).T
     sent.extend(copies)
-    sent.extend(leaving.values())
 
     for j, (buf, k) in enumerate(((nsq, 7), (lsq, 31))):
         ref = buf.at[pl.ds(0, k)]

time: 113 us -> 107 us (0.947)
  Pallas kernels: 108 us -> 103 us
    pallas_call x1, Pallas kernels: 108 us -> 103 us  [per_device(): pl.pallas_call(body, out_shape=(jax.ShapeDtypeStruct((4, LANE), F32), jax...]
where the time goes in v5:
time: 107 us
  Pallas kernels  103 us (96%)
  local copies, waits for them, and re-layouts  3.44 us (3%)
    pallas_call x1, Pallas kernels, per_device(): pl.pallas_call(body, out_shape=(jax.ShapeDtypeStruct((4, LANE), F32), jax...  103 us
    unnamed x7, local copies, waits for them, and re-layouts  3.44 us

profile of v5, /device:TPU:2, one launch (start us, length us, event | category | flops | bytes accessed | tf_op | source)
XLA Modules:
  0.0 107.1 jit_solution(17301062560132054942)
XLA Ops:
  0.6 0.0 copy-start
  0.6 0.9 copy-done
  1.5 0.0 copy-start.1
  1.5 0.7 copy-done.1
  2.2 103.0 %shard_map.58 = (f32[4,128]{1,0:T(4,128)S(1)}, f32[4,128]{1,0:T(4,128)S(1)}, f32[128,512]{1,0:T(8,128)S(1)}) custom-call(bf16[512,512]{1,0:T(8,128)(2,1)} %refs_0_.1, bf16[512,128]{1,0:T(8,128)(2,1)S(1)} %copy-done, f32[4,128]{1,0:T(4,128)S(1)} %bitcast.3), custom_call_target="tpu_custom_call" | custom-call | tf_op jit(solution)/shard_map/pallas_call | solution.py:528
  105.2 0.6 copy.9
  105.8 0.6 copy.10
  106.4 0.7 copy.11
Async XLA Ops:
  0.6 0.9 copy-start
  1.5 0.7 copy-start.1

commit v6 on v5

--- a/solution.py
+++ b/solution.py
@@ -151,8 +151,6 @@
     first_dn = nsend(col, 1, 3, y_dn, own_half(1))
 
     sent.append(lat_x)
-    xh_send(0, 0)
-    xh_send(0, 1)
 
     own_n.wait()
     own_l.wait()
@@ -167,6 +165,8 @@
     lwait(lat(0, 1), 0)
     lsend(lat(0, 1), 2, z_up)
     lsend(lat(0, 1), 10, z_dn)
+    xh_send(0, 0)
+    xh_send(0, 1)
     lat_forward(1, 0, z_dirs)
     lsend(own_pair, 17, other_core)
 

time: 107 us -> 108 us (level)
  no operation moved by 1% of the time
where the time goes in v6:
time: 108 us; the launch traced here: 107 us
  Pallas kernels  103 us (95%)
  local copies, waits for them, and re-layouts  3.44 us (3%)
    pallas_call x1, Pallas kernels, per_device(): pl.pallas_call(body, out_shape=(jax.ShapeDtypeStruct((4, LANE), F32), jax...  103 us
    unnamed x7, local copies, waits for them, and re-layouts  3.44 us

profile of v6, /device:TPU:2, one launch (start us, length us, event | category | flops | bytes accessed | tf_op | source)
XLA Modules:
  0.0 107.2 jit_solution(7001759248728432024)
XLA Ops:
  0.6 0.0 copy-start
  0.6 0.9 copy-done
  1.5 0.0 copy-start.1
  1.5 0.7 copy-done.1
  2.2 103.1 %shard_map.58 = (f32[4,128]{1,0:T(4,128)S(1)}, f32[4,128]{1,0:T(4,128)S(1)}, f32[128,512]{1,0:T(8,128)S(1)}) custom-call(bf16[512,512]{1,0:T(8,128)(2,1)} %refs_0_.1, bf16[512,128]{1,0:T(8,128)(2,1)S(1)} %copy-done, f32[4,128]{1,0:T(4,128)S(1)} %bitcast.3), custom_call_target="tpu_custom_call" | custom-call | tf_op jit(solution)/shard_map/pallas_call | solution.py:528
  105.4 0.6 copy.9
  105.9 0.6 copy.10
  106.5 0.7 copy.11
Async XLA Ops:
  0.6 0.9 copy-start
  1.5 0.7 copy-start.1

commit v7 on v6

--- a/solution.py
+++ b/solution.py
@@ -138,6 +138,8 @@
             lwait(block, 1 + 8 * dr + 2 * (step - 1) + part)
             if step < 3 or part == dr:
                 lsend(block, 1 + 8 * dr + 2 * step + part, dev)
+            if step == 3 and part == dr:
+                lsend(block, 24 + part, (dev[0] + 1 - 2 * core, col))
 
     def lat_share(step):
         for dr, sgn, _ in z_dirs:
@@ -151,6 +153,7 @@
     first_dn = nsend(col, 1, 3, y_dn, own_half(1))
 
     sent.append(lat_x)
+    xh_send(0, 0)
 
     own_n.wait()
     own_l.wait()
@@ -165,7 +168,6 @@
     lwait(lat(0, 1), 0)
     lsend(lat(0, 1), 2, z_up)
     lsend(lat(0, 1), 10, z_dn)
-    xh_send(0, 0)
     xh_send(0, 1)
     lat_forward(1, 0, z_dirs)
     lsend(own_pair, 17, other_core)
@@ -220,9 +222,10 @@
     lat_share(3)
     lwait(lat(4, 0), 7)
     lwait(lat(4, 1), 16)
-    lsend(lt.at[ring_z(4), core], 24, other_core)
-    for j, d in enumerate((0, -1, 1, -2, 2, -3, 3, 4)):
+    for j, d in enumerate((0, -1, 1, -2, 2, -3, 3)):
         lwait(lt.at[ring_z(d), 1 - core], 17 + j)
+    lwait(lt.at[ring_z(4), 1 - core, xl], 24)
+    lwait(lt.at[ring_z(4), 1 - core, 1 - xl], 25)
 
     def accumulate(slot):
         a = nz[slot]
@@ -557,7 +560,7 @@
             dma((2,)), dma((2,)),
             dma((12,)), dma((12,)),
             dma((2, 2)), dma((2, 2)),
-            dma((25,)), dma((25,)),
+            dma((26,)), dma((26,)),
             dma((2,)), dma((2,)),
             dma((4,)), dma((4,)),
             dma((2, Z)), dma((2, Z)),

time: 108 us -> 108 us (level)
  no operation moved by 1% of the time
where the time goes in v7:
time: 108 us; the launch traced here: 107 us
  Pallas kernels  103 us (95%)
  local copies, waits for them, and re-layouts  3.44 us (3%)
    pallas_call x1, Pallas kernels, per_device(): pl.pallas_call(body, out_shape=(jax.ShapeDtypeStruct((4, LANE), F32), jax...  103 us
    unnamed x7, local copies, waits for them, and re-layouts  3.44 us

profile of v7, /device:TPU:2, one launch (start us, length us, event | category | flops | bytes accessed | tf_op | source)
XLA Modules:
  0.0 107.4 jit_solution(16529478782486613341)
XLA Ops:
  0.6 0.0 copy-start
  0.6 0.9 copy-done
  1.5 0.0 copy-start.1
  1.5 0.7 copy-done.1
  2.2 103.3 %shard_map.58 = (f32[4,128]{1,0:T(4,128)S(1)}, f32[4,128]{1,0:T(4,128)S(1)}, f32[128,512]{1,0:T(8,128)S(1)}) custom-call(bf16[512,512]{1,0:T(8,128)(2,1)} %refs_0_.1, bf16[512,128]{1,0:T(8,128)(2,1)S(1)} %copy-done, f32[4,128]{1,0:T(4,128)S(1)} %bitcast.3), custom_call_target="tpu_custom_call" | custom-call | tf_op jit(solution)/shard_map/pallas_call | solution.py:531
  105.6 0.6 copy.9
  106.2 0.6 copy.10
  106.7 0.7 copy.11
Async XLA Ops:
  0.6 0.9 copy-start
  1.5 0.7 copy-start.1

commit v8 on v7

--- a/solution.py
+++ b/solution.py
@@ -191,10 +191,6 @@
 
     lat_forward(1, 1, z_dirs)
     lat_share(1)
-    for peer in col_peers:
-        rc(nsq.at[col], nsq.at[col], q_send.at[0], q_recv.at[0], peer).start()
-    for peer in row_peers:
-        rc(lsq.at[row], lsq.at[row], q_send.at[1], q_recv.at[1], peer).start()
     lat_forward(2, 0, z_dirs)
     lat_forward(2, 1, z_dirs)
     lat_share(2)
@@ -220,6 +216,10 @@
 
     lat_forward(3, 1, z_dirs)
     lat_share(3)
+    for peer in col_peers:
+        rc(nsq.at[col], nsq.at[col], q_send.at[0], q_recv.at[0], peer).start()
+    for peer in row_peers:
+        rc(lsq.at[row], lsq.at[row], q_send.at[1], q_recv.at[1], peer).start()
     lwait(lat(4, 0), 7)
     lwait(lat(4, 1), 16)
     for j, d in enumerate((0, -1, 1, -2, 2, -3, 3)):

time: 108 us -> 107 us (level)
  no operation moved by 1% of the time
where the time goes in v8:
time: 107 us
  Pallas kernels  103 us (96%)
  local copies, waits for them, and re-layouts  3.44 us (3%)
    pallas_call x1, Pallas kernels, per_device(): pl.pallas_call(body, out_shape=(jax.ShapeDtypeStruct((4, LANE), F32), jax...  103 us
    unnamed x7, local copies, waits for them, and re-layouts  3.44 us

profile of v8, /device:TPU:2, one launch (start us, length us, event | category | flops | bytes accessed | tf_op | source)
XLA Modules:
  0.0 106.7 jit_solution(13179564084376347742)
XLA Ops:
  0.6 0.0 copy-start
  0.6 0.9 copy-done
  1.5 0.0 copy-start.1
  1.5 0.7 copy-done.1
  2.2 102.7 %shard_map.58 = (f32[4,128]{1,0:T(4,128)S(1)}, f32[4,128]{1,0:T(4,128)S(1)}, f32[128,512]{1,0:T(8,128)S(1)}) custom-call(bf16[512,512]{1,0:T(8,128)(2,1)} %refs_0_.1, bf16[512,128]{1,0:T(8,128)(2,1)S(1)} %copy-done, f32[4,128]{1,0:T(4,128)S(1)} %bitcast.3), custom_call_target="tpu_custom_call" | custom-call | tf_op jit(solution)/shard_map/pallas_call | solution.py:531
  104.9 0.6 copy.9
  105.5 0.6 copy.10
  106.0 0.7 copy.11
Async XLA Ops:
  0.6 0.9 copy-start
  1.5 0.7 copy-start.1
